TPU v7x, 512 devices: a whole 4x8x8 slice. The times are simulated.
512 devices in a mesh: dp: 128 (over y_lo, x, z), mp: 4 (over y_hi, core).
Axes of the slice: x: 4, y: 8 (y_hi: 2, y_lo: 4; y = y_hi * 4 + y_lo), z: 8, core: 2. Of those that a mesh axis runs over, the one named last changes fastest.
Arguments:
- features: bfloat16 [16384, 1536], P('dp', 'mp'), may hold values from -240 to 240
- proj_weight: bfloat16 [1536, 1152], P('mp'), may hold values from -0.15625 to 0.15625
- texts: bfloat16 [16384, 1152], P(('dp', 'mp')), may hold values from -6 to 6
Outputs:
- grad_features: bfloat16 [16384, 1536], P('dp', 'mp')
- grad_weight: float32 [1536, 1152], P('mp')
All inputs are finite; a program needn't handle non-finite values.
Results may differ from a plain program's by a relative error of at most 0.011.
Values may be sent and summed in bfloat16 or wider, within the bound.
A program may use at most 64 MiB of HBM per device.

v0:
```python
import jax
import jax.numpy as jnp
from jax import lax
from jax.sharding import PartitionSpec as P

logit_scale = 100.0
logit_bias = -10.0
epsilon = 1e-06


def unit_rows(values):
    return values * lax.rsqrt(jnp.sum(values * values, axis=1, keepdims=True) + epsilon)


def add_texts(unit_img_b, image_ids, piece, piece_ids):
    unit_txt_b = unit_rows(piece.astype(jnp.float32)).astype(jnp.bfloat16)
    logits = (
        logit_scale * jnp.dot(unit_img_b, unit_txt_b.T, preferred_element_type=jnp.float32)
        + logit_bias
    )
    labels = jnp.where(image_ids[:, None] == piece_ids[None, :], 1.0, -1.0).astype(jnp.float32)
    slopes = (-labels * jax.nn.sigmoid(-labels * logits)).astype(jnp.bfloat16)
    return logit_scale * jnp.dot(slopes, unit_txt_b, preferred_element_type=jnp.float32)


def shards(features, proj_weight, texts):
    local_rows = features.shape[0]
    width_local = features.shape[1]
    mp_count = lax.axis_size("mp")
    full_width = width_local * mp_count
    mp_index = lax.axis_index("mp")
    dp_index = lax.axis_index("dp")
    text_rows = texts.shape[0]
    inputs = features.astype(jnp.float32)
    mean_in = lax.psum(jnp.sum(inputs, axis=1, keepdims=True), "mp") / full_width
    centred = inputs - mean_in
    normed_b = centred.astype(jnp.bfloat16)
    partial_proj = jnp.dot(normed_b, proj_weight, preferred_element_type=jnp.float32)
    project = lax.psum(partial_proj, "mp")
    inv_norm = lax.rsqrt(jnp.sum(project * project, axis=1, keepdims=True) + epsilon)
    unit_img = project * inv_norm
    unit_img_b = unit_img.astype(jnp.bfloat16)
    image_ids = dp_index * local_rows + jnp.arange(local_rows, dtype=jnp.int32)
    piece = lax.all_gather(texts, "dp", axis=0, tiled=True)
    positions = jnp.arange(piece.shape[0], dtype=jnp.int32)
    shard_of = positions // text_rows
    piece_ids = (shard_of * mp_count + mp_index) * text_rows + positions % text_rows
    grad_unit = add_texts(unit_img_b, image_ids, piece, piece_ids)
    grad_unit = lax.psum(grad_unit, "mp")
    grad_proj = inv_norm * (
        grad_unit - unit_img * jnp.sum(unit_img * grad_unit, axis=1, keepdims=True)
    )
    grad_proj_b = grad_proj.astype(jnp.bfloat16)
    weight_part = jnp.dot(normed_b.T, grad_proj_b, preferred_element_type=jnp.float32)
    grad_weight = lax.psum(weight_part, "dp")
    grad_normed = jnp.dot(grad_proj_b, proj_weight.T, preferred_element_type=jnp.float32)
    grad_total = lax.psum(jnp.sum(grad_normed, axis=1, keepdims=True), "mp")
    grad_in = grad_normed - grad_total / full_width
    return (grad_in.astype(jnp.bfloat16), grad_weight)


def solution(mesh):
    return jax.shard_map(
        shards,
        mesh=mesh,
        in_specs=(P("dp", "mp"), P("mp", None), P(("dp", "mp"), None)),
        out_specs=(P("dp", "mp"), P("mp", None)),
        check_vma=False,
    )
```

profile of v0, /device:TPU:32, one launch (start us, length us, event | category | flops | bytes accessed | tf_op | source)
XLA Modules:
  0.0 2207.1 jit_solution(18278150930301885179)
XLA Ops:
  8.0 0.0 copy-start
  8.0 0.0 all-reduce.4.cloned.1.call-start
  8.1 1.1 convert_reduce_fusion
  9.1 9.6 psum.35
  18.7 0.0 copy-done
  18.7 2.1 fusion.32
  20.8 0.0 all-reduce.4.cloned.1.call-update
  20.8 0.0 all-gather.2.cloned.1.call-start
  20.9 0.5 all-gather.2.cloned.1.call-update
  21.4 0.0 all-reduce.6.cloned.1.call-start
  21.5 64.7 %all-reduce.4.cloned.1.call-done = f32[128,1152]{1,0:T(8,128)} async-done(((f32[128,1152]{1,0:T(8,128)}), f32[128,1152]{1,0:T(8,128)}) %all-reduce.4.cloned.1.call-update) | async-done | bytes 589840 | tf_op jit(solution)/shard_map/psum | solution.py:39
  86.1 1.2 multiply_reduce_fusion.1
  87.3 0.0 copy-start.1
  87.3 649.3 %all-gather.2.cloned.1.call-done = bf16[4096,1152]{1,0:T(8,128)(2,1)} async-done(((bf16[32,1152]{1,0:T(8,128)(2,1)}), bf16[4096,1152]{1,0:T(8,128)(2,1)}) %all-gather.2.cloned.1.call-update) | async-done | bytes 9437200 | tf_op jit(solution)/shard_map/all_gather | solution.py:44
  736.6 5.6 fusion
  742.2 0.0 copy-done.1
  742.2 12.9 fusion.13
  755.1 0.0 copy-start.2
  755.1 0.0 all-reduce.6.cloned.1.call-update
  755.1 0.0 all-reduce.8.cloned.1.call-start
  755.2 55.3 %all-reduce.6.cloned.1.call-done = f32[128,1152]{1,0:T(8,128)} async-done(((f32[128,1152]{1,0:T(8,128)}), f32[128,1152]{1,0:T(8,128)}) %all-reduce.6.cloned.1.call-update) | async-done | bytes 589840 | tf_op jit(solution)/shard_map/psum | solution.py:49
  810.5 1.3 multiply_reduce_fusion
  811.7 1.2 multiply_convert_fusion
  813.0 0.0 copy-done.2
  813.0 1.7 fusion.30
  814.7 0.0 all-reduce.8.cloned.1.call-update
  814.7 0.5 fusion.49
  815.2 12.9 psum.38
  828.1 0.7 subtract_convert_fusion
  828.8 1368.1 %all-reduce.8.cloned.1.call-done = f32[384,1152]{1,0:T(8,128)} async-done(((f32[384,1152]{1,0:T(8,128)}), f32[384,1152]{1,0:T(8,128)}) %all-reduce.8.cloned.1.call-update) | async-done | bytes 1769488 | tf_op jit(solution)/shard_map/psum | solution.py:55
  2196.9 2.8 copy.8
  (6 shorter events, 0.0 us)
Async XLA Ops:
  8.0 10.7 copy-start
  8.0 78.1 %all-reduce.4.cloned.1.call-start = ((), (), s32[]{:S(2)}) async-start(), calls=%async_computation | async-start | bytes 1179648 | tf_op jit(solution)/shard_map/psum | solution.py:39
  20.8 715.8 %all-gather.2.cloned.1.call-start = ((), (), s32[]{:S(2)}) async-start(), calls=%async_computation.1 | async-start | bytes 9510912 | tf_op jit(solution)/shard_map/all_gather | solution.py:44
  21.4 789.0 %all-reduce.6.cloned.1.call-start = ((), (), s32[]{:S(2)}) async-start(), calls=%async_computation.2 | async-start | bytes 1179648 | tf_op jit(solution)/shard_map/psum | solution.py:49
  87.3 654.9 %copy-start.1 = (f32[128,1152]{1,0:T(8,128)S(1)}, f32[128,1152]{1,0:T(8,128)}, u32[]{:S(2)}) copy-start(f32[128,1152]{1,0:T(8,128)} %all-reduce.4.cloned.1.call-done) | copy-start | bytes 1769476
  755.1 57.9 %copy-start.2 = (bf16[128,384]{1,0:T(8,128)(2,1)S(1)}, bf16[128,384]{1,0:T(8,128)(2,1)}, u32[]{:S(2)}) copy-start(bf16[128,384]{1,0:T(8,128)(2,1)} %param.3) | copy-start | bytes 294916
  755.1 1441.8 %all-reduce.8.cloned.1.call-start = ((), (), s32[]{:S(2)}) async-start(), calls=%async_computation.3 | async-start | bytes 3538944 | tf_op jit(solution)/shard_map/psum | solution.py:55
Sparse Core Ops, SparseCore 0:
  21.0 65.1 all-reduce.3
  755.3 55.1 all-reduce.5
Sparse Core Ops, SparseCore 1:
  23.4 713.2 all-gather.1
  814.8 1382.1 all-reduce.7
where the time goes:
time: 2210 us
  waiting for transfers between devices  2140 us (97%)
  blocking collectives  22.5 us (1%)
    psum x1, waiting for transfers between devices, shards(): grad_weight = lax.psum(weight_part, 'dp')  1370 us
    all_gather x1, waiting for transfers between devices, shards(): piece = lax.all_gather(texts, 'dp', axis=0, tiled=True)  649 us
    psum x1, waiting for transfers between devices, shards(): project = lax.psum(partial_proj, 'mp')  64.7 us
    psum x1, waiting for transfers between devices, shards(): grad_unit = lax.psum(grad_unit, 'mp')  55.3 us
  transfers between devices with their start and end apart: 4, of which 4 were waited for; matrix products, arithmetic and copies ran while one was open for 0% of the time, Pallas kernels for 0%

commit v1 on v0

v1 whole, which is shorter than its diff:
```python
import jax
import jax.numpy as jnp
from jax import lax
from jax.experimental import pallas as pl
from jax.experimental.pallas import tpu as pltpu
from jax.sharding import PartitionSpec as P

logit_scale = 100.0
logit_bias = -10.0
epsilon = 1e-06
NX, NYL, NZ = 4, 4, 8
NY = 2 * NYL
MESH = pl.DeviceIdType.MESH
NT = (((1,), (1,)), ((), ()))


def place(x, y, z, c):
    return ((y % NYL) * NX + x) * NZ + z, (y // NYL) * 2 + c


def unit_scale(values):
    return lax.rsqrt(jnp.sum(values * values, axis=1, keepdims=True) + epsilon)


def tile_slots():
    slots = []
    for i in range(6):
        for j in range(9):
            q = i * 9 + j
            slots.append((i, j, q % NX, (q // NX) % NZ, q // (NX * NZ)))
    return slots


def kernel(
    feat_ref, w_ref, text_ref, gfeat_ref, gweight_ref,
    txt, sums, cols, normed, nt_send, nt, part, part_core, part_far, unit, img,
    grad, grad_core, half_send, half_recv, gproj, wsend, wx, zsend, wz, fin,
    tx_s, tx_r, tz_s, tz_r, su_s, su_r, co_s, co_r, nt_s, nt_r, pc_s, pc_r, im_s, im_r,
    gc_s, gc_r, gy_s, gy_r, gp_s, gp_r, wx_s, wx_r, wz_s, wz_r, fy_s, fy_r, fz_s, fz_r, fx_s, fx_r,
):
    dp = lax.axis_index("dp")
    mp = lax.axis_index("mp")
    yl = dp // (NX * NZ)
    x = (dp // NZ) % NX
    z = dp % NZ
    yh = mp // 2
    c = mp % 2
    y = yh * NYL + yl
    sib = place(x, y, z, 1 - c)
    y_far = (y + NYL) % NY
    far = place(x, y_far, z, c)
    far_sib = place(x, y_far, z, 1 - c)

    def on_y(k):
        return place(x, (y + k) % NY, z, c)

    def on_yl(k):
        return place(x, yh * NYL + (yl + k) % NYL, z, c)

    def on_x(k):
        return place((x + k) % NX, y, z, c)

    def on_z(k):
        return place(x, y, (z + k) % NZ, c)

    def send(src, dst, s, r, to):
        copy = pltpu.make_async_remote_copy(
            src_ref=src, dst_ref=dst, send_sem=s, recv_sem=r, device_id=to, device_id_type=MESH
        )
        copy.start()
        return copy

    barrier = pltpu.get_barrier_semaphore()
    others = [sib, far_sib]
    others += [on_y(k) for k in range(1, NY)]
    others += [on_x(k) for k in range(1, NX)]
    others += [on_z(k) for k in range(1, NZ)]
    for other in others:
        pl.semaphore_signal(barrier, inc=1, device_id=other, device_id_type=MESH)

    text = text_ref[...].astype(jnp.float32)
    txt[z, x] = (text * unit_scale(text)).astype(jnp.bfloat16)
    inputs = feat_ref[...].astype(jnp.float32)
    row_sum = jnp.sum(inputs, axis=1, keepdims=True)
    sums[mp] = jnp.broadcast_to(row_sum, (128, 128)).T[:8]
    weights = w_ref[...]
    cols[mp] = jnp.broadcast_to(
        jnp.sum(weights.astype(jnp.float32), axis=0, keepdims=True), (8, weights.shape[1])
    )
    pl.semaphore_wait(barrier, len(others))

    mates = [sib, far, far_sib]
    sum_copies = [send(sums.at[mp], sums.at[mp], su_s.at[k], su_r.at[k], to) for k, to in enumerate(mates)]
    text_copies = [
        send(txt.at[z, x], txt.at[z, x], tx_s.at[k - 1], tx_r.at[k - 1], on_x(k)) for k in range(1, NX)
    ]
    col_copies = [send(cols.at[mp], cols.at[mp], co_s.at[k], co_r.at[k], to) for k, to in enumerate(mates)]

    def text_step(step, before):
        for copy in before:
            copy.wait()
        copies = []
        for way, d in enumerate((1, -1)):
            slot = (z - d * (step - 1) + 2 * NZ) % NZ
            block = txt.at[slot]
            if step == NZ // 2:
                block = txt.at[slot, pl.ds(way * (NX // 2), NX // 2)]
            index = (step - 1) * 2 + way
            copies.append(send(block, block, tz_s.at[index], tz_r.at[index], on_z((d + NZ) % NZ)))
        return copies

    for copy in sum_copies:
        copy.wait()
    total = (sums[0] + sums[1]) + (sums[2] + sums[3])
    mean_in = jnp.broadcast_to(total[:1] / 1536.0, (128, 128)).T[:, :1]
    centred = inputs - mean_in
    normed[...] = centred.astype(jnp.bfloat16)
    ring = text_step(1, text_copies)
    partial = jnp.dot(normed[...], weights, preferred_element_type=jnp.float32)
    for h in range(2):
        for b in range(2):
            part[b, h] = partial[(h * 2 + b) * 32 : (h * 2 + b + 1) * 32]
    core_copy = send(part.at[1 - c], part_core, pc_s.at[0], pc_r.at[0], sib)
    turned = centred.T.astype(jnp.bfloat16)
    for g in range(NYL):
        nt_send[g] = turned[g * 96 : (g + 1) * 96]
    nt[yl] = nt_send[yl]
    core_copy.wait()
    part[c, 1 - yh] += part_core[1 - yh]
    far_copy = send(part.at[c, 1 - yh], part_far, pc_s.at[1], pc_r.at[1], far)
    nt_copies = [
        send(nt_send.at[(yl + k) % NYL], nt.at[yl], nt_s.at[k - 1], nt_r.at[k - 1], on_yl(k))
        for k in range(1, NYL)
    ]
    ring = text_step(2, ring)
    far_copy.wait()
    project = part[c, yh] + part_core[yh] + part_far[...]
    inv_norm = unit_scale(project)
    unit_img = project * inv_norm
    unit[...] = unit_img
    img[c, y] = unit_img.astype(jnp.bfloat16)
    img_copies = [
        send(img.at[c, y], img.at[c, y], im_s.at[k], im_r.at[k], on_y(k)) for k in range(1, NY)
    ]
    ring = text_step(3, ring)
    for copy in img_copies:
        copy.wait()
    img_core = send(img.at[c], img.at[c], im_s.at[0], im_r.at[0], sib)
    ring = text_step(4, ring)
    grad[...] = jnp.zeros_like(grad)
    img_core.wait()
    for copy in ring:
        copy.wait()

    @pl.loop(0, NZ // 2)
    def _(b):
        texts = txt[pl.ds(b * 2, 2)].reshape(2 * NX * 32, -1)
        images = img[...].reshape(2 * NY * 32, -1)
        score = lax.dot_general(images, texts, NT, preferred_element_type=jnp.float32)
        logits = logit_scale * score + logit_bias
        rows = lax.broadcasted_iota(jnp.int32, logits.shape, 0)
        columns = lax.broadcasted_iota(jnp.int32, logits.shape, 1) + b * (2 * NX * 32)
        same = rows - (c * NY + y) * 32 == columns - (z * NX + x) * 32
        own = (rows // 32) == (c * NY + y)
        same = jnp.logical_and(same, own)
        slope = jax.nn.sigmoid(jnp.where(same, -logits, logits))
        slope = jnp.where(same, -slope, slope).astype(jnp.bfloat16)
        grad[...] += jnp.dot(slope, texts, preferred_element_type=jnp.float32).reshape(grad.shape)

    grad_core_copy = send(grad.at[1 - c], grad_core, gc_s.at[0], gc_r.at[0], sib)
    grad_core_copy.wait()
    summed = grad[c] + grad_core[...]
    grad[c] = summed
    half_send[...] = summed.astype(jnp.bfloat16)
    half_copies = [
        send(half_send.at[(y + k) % NY], half_recv.at[y], gy_s.at[k - 1], gy_r.at[k - 1], on_y(k))
        for k in range(1, NY)
    ]
    half_recv[y] = jnp.zeros(half_recv.shape[1:], half_recv.dtype)
    grad_unit = grad[c, y]
    for copy in half_copies:
        copy.wait()
    for k in range(NY):
        grad_unit = grad_unit + half_recv[k].astype(jnp.float32)
    grad_unit = logit_scale * grad_unit
    unit_img = unit[...]
    along = jnp.sum(unit_img * grad_unit, axis=1, keepdims=True)
    gproj[c, y] = (inv_norm * (grad_unit - unit_img * along)).astype(jnp.bfloat16)
    gp_copies = [
        send(gproj.at[c, y], gproj.at[c, y], gp_s.at[k], gp_r.at[k], on_y(k)) for k in range(1, NY)
    ]
    wsend[...] = jnp.zeros_like(wsend)
    for copy in col_copies + nt_copies:
        copy.wait()
    for copy in gp_copies:
        copy.wait()
    gp_core = send(gproj.at[c], gproj.at[c], gp_s.at[0], gp_r.at[0], sib)
    gp_core.wait()

    def group_rows(g):
        return jnp.concatenate([gproj[0, g], gproj[1, g], gproj[0, g + NYL], gproj[1, g + NYL]], axis=0)

    weight_part = jnp.dot(nt[0], group_rows(0), preferred_element_type=jnp.float32)
    for g in range(1, NYL):
        weight_part += jnp.dot(nt[g], group_rows(g), preferred_element_type=jnp.float32)
    weight_part = weight_part.astype(jnp.bfloat16)
    slots = tile_slots()
    for i, j, tx, tz, k in slots:
        wsend[tx, tz, k] = weight_part[i * 16 : (i + 1) * 16, j * 128 : (j + 1) * 128]
    wx_copies = [
        send(wsend.at[(x + k) % NX], wx.at[x], wx_s.at[k - 1], wx_r.at[k - 1], on_x(k)) for k in range(1, NX)
    ]
    rows = group_rows(yl)
    grad_normed = lax.dot_general(rows, weights, NT, preferred_element_type=jnp.float32)
    col = (cols[0] + cols[1]) + (cols[2] + cols[3])
    grad_total = jnp.sum(rows.astype(jnp.float32) * col[:1], axis=1, keepdims=True)
    gfeat_ref[...] = (grad_normed - grad_total / 1536.0).astype(jnp.bfloat16)
    wx[x] = wsend[x]
    for copy in wx_copies:
        copy.wait()
    over_x = wx[0].astype(jnp.float32)
    for k in range(1, NX):
        over_x += wx[k].astype(jnp.float32)
    zsend[...] = over_x.astype(jnp.bfloat16)
    wz_copies = [
        send(zsend.at[(z + k) % NZ], wz.at[z], wz_s.at[k - 1], wz_r.at[k - 1], on_z(k)) for k in range(1, NZ)
    ]
    wz[z] = zsend[z]
    for copy in wz_copies:
        copy.wait()
    over_z = wz[0].astype(jnp.float32)
    for k in range(1, NZ):
        over_z += wz[k].astype(jnp.float32)
    fin[x, z, yl] = over_z.astype(jnp.bfloat16)
    for copy in [
        send(fin.at[x, z, yl], fin.at[x, z, yl], fy_s.at[k - 1], fy_r.at[k - 1], on_yl(k))
        for k in range(1, NYL)
    ]:
        copy.wait()
    for copy in [
        send(fin.at[x, z], fin.at[x, z], fz_s.at[k - 1], fz_r.at[k - 1], on_z(k)) for k in range(1, NZ)
    ]:
        copy.wait()
    for copy in [send(fin.at[x], fin.at[x], fx_s.at[k - 1], fx_r.at[k - 1], on_x(k)) for k in range(1, NX)]:
        copy.wait()
    for g in range(NYL):
        for i, j, tx, tz, k in slots:
            gweight_ref[g * 96 + i * 16 : g * 96 + (i + 1) * 16, j * 128 : (j + 1) * 128] = fin[tx, tz, g, k]


def shards(features, proj_weight, texts):
    rows, width = features.shape
    e = proj_weight.shape[1]
    bf16, f32 = jnp.bfloat16, jnp.float32
    dma = pltpu.SemaphoreType.DMA
    counts = [NX - 1, NZ, 3, 3, NYL - 1, 2, NY, 1, NY - 1, NY, NX - 1, NZ - 1, NYL - 1, NZ - 1, NX - 1]
    semaphores = [dma((n,)) for n in counts for _ in range(2)]
    grad_features, grad_weight = pl.pallas_call(
        kernel,
        out_shape=(
            jax.ShapeDtypeStruct((rows, width), bf16),
            jax.ShapeDtypeStruct((width, e), bf16),
        ),
        in_specs=[pl.BlockSpec(memory_space=pltpu.VMEM)] * 3,
        out_specs=[pl.BlockSpec(memory_space=pltpu.VMEM)] * 2,
        scratch_shapes=[
            pltpu.VMEM((NZ, NX, 32, e), bf16),
            pltpu.VMEM((4, 8, 128), f32),
            pltpu.VMEM((4, 8, e), f32),
            pltpu.VMEM((rows, width), bf16),
            pltpu.VMEM((NYL, width // NYL, rows), bf16),
            pltpu.VMEM((NYL, width // NYL, rows), bf16),
            pltpu.VMEM((2, 2, 32, e), f32),
            pltpu.VMEM((2, 32, e), f32),
            pltpu.VMEM((32, e), f32),
            pltpu.VMEM((32, e), f32),
            pltpu.VMEM((2, NY, 32, e), bf16),
            pltpu.VMEM((2, NY, 32, e), f32),
            pltpu.VMEM((NY, 32, e), f32),
            pltpu.VMEM((NY, 32, e), bf16),
            pltpu.VMEM((NY, 32, e), bf16),
            pltpu.VMEM((2, NY, 32, e), bf16),
            pltpu.VMEM((NX, NZ, 2, 16, 128), bf16),
            pltpu.VMEM((NX, NZ, 2, 16, 128), bf16),
            pltpu.VMEM((NZ, 2, 16, 128), bf16),
            pltpu.VMEM((NZ, 2, 16, 128), bf16),
            pltpu.VMEM((NX, NZ, NYL, 2, 16, 128), bf16),
        ]
        + semaphores,
        compiler_params=pltpu.CompilerParams(
            collective_id=0, has_side_effects=True, vmem_limit_bytes=48 << 20
        ),
        cost_estimate=pl.CostEstimate(flops=2_750_000_000, bytes_accessed=8_000_000, transcendentals=524288),
        name="head_loss",
    )(features, proj_weight, texts)
    return grad_features, grad_weight.astype(f32)


def solution(mesh):
    return jax.shard_map(
        shards,
        mesh=mesh,
        in_specs=(P("dp", "mp"), P("mp", None), P(("dp", "mp"), None)),
        out_specs=(P("dp", "mp"), P("mp", None)),
        check_vma=False,
    )
```

time: 2210 us -> 137 us (0.06)
  the two profiles are of different devices: /device:TPU:32 before, /device:TPU:8 now
where the time goes in v1:
time: 137 us
  Pallas kernels  131 us (96%)
  local copies, waits for them, and re-layouts  3.58 us (3%)
    pallas_call x1, Pallas kernels, shards(): pl.pallas_call(kernel, out_shape=(jax.ShapeDtypeStruct((rows, width), bf1...  131 us
    unnamed x7, local copies, waits for them, and re-layouts  3.58 us

profile of v1, /device:TPU:8, one launch (start us, length us, event | category | flops | bytes accessed | tf_op | source)
XLA Modules:
  0.0 136.7 jit_solution(14770916958896405227)
XLA Ops:
  0.6 0.0 copy-start
  0.6 1.2 copy-done
  1.8 0.0 copy-start.1
  1.8 0.9 copy-done.1
  2.7 0.0 copy-start.2
  2.7 0.9 copy-done.2
  3.6 131.2 %head_loss.1 = (bf16[128,384]{1,0:T(8,128)(2,1)S(1)}, bf16[384,1152]{1,0:T(8,128)(2,1)S(1)}) custom-call(bf16[128,384]{1,0:T(8,128)(2,1)S(1)} %copy-done.1, bf16[384,1152]{1,0:T(8,128)(2,1)S(1)} %copy-done, bf16[32,1152]{1,0:T(8,128)(2,1)S(1)} %copy-done.2), custom_call_target="tpu_custom_call" | custom-call | flops 2750000128 | bytes 8000000 | tf_op jit(solution)/shard_map/head_loss/pallas_call | solution.py:258
  134.8 1.3 convert_element_type.3
  136.1 0.6 copy.6
Async XLA Ops:
  0.6 1.2 copy-start
  1.8 0.9 copy-start.1
  2.7 0.9 copy-start.2

commit v2 on v1

v2 whole, which is shorter than its diff:
```python
import jax
import jax.numpy as jnp
from jax import lax
from jax.experimental import pallas as pl
from jax.experimental.pallas import tpu as pltpu
from jax.sharding import PartitionSpec as P

logit_scale = 100.0
logit_bias = -10.0
epsilon = 1e-06
NX, NYL, NZ = 4, 4, 8
NY = 2 * NYL
MESH = pl.DeviceIdType.MESH
NT = (((1,), (1,)), ((), ()))


def place(x, y, z, c):
    return ((y % NYL) * NX + x) * NZ + z, (y // NYL) * 2 + c


def unit_scale(values):
    return lax.rsqrt(jnp.sum(values * values, axis=1, keepdims=True) + epsilon)


def tile_slots():
    slots = []
    for i in range(6):
        for j in range(9):
            q = i * 9 + j
            slots.append((i, j, q % NX, (q // NX) % NZ, q // (NX * NZ)))
    return slots


def remote(src, dst, s, r, to):
    copy = pltpu.make_async_remote_copy(
        src_ref=src, dst_ref=dst, send_sem=s, recv_sem=r, device_id=to, device_id_type=MESH
    )
    copy.start()
    return copy


def wait_all(copies):
    for copy in copies:
        copy.wait()


def share(at, me, count, to, s, r):
    def go(index, k):
        return remote(at(me, None), at(me, None), s.at[index], r.at[index], to(k))

    return [go(0, 2), go(1, count - 2), go(2, 1), go(3, count - 1)]


def pass_on(at, me, count, to, s, r, copies):
    low = (me + count - 2) % count
    high = (me + 2) % count
    copies[0].wait_recv()
    on = [
        remote(at(low, None), at(low, None), s.at[4], r.at[4], to(1)),
        remote(at(low, 0), at(low, 0), s.at[5], r.at[5], to(2)),
    ]
    copies[1].wait_recv()
    on += [
        remote(at(high, None), at(high, None), s.at[6], r.at[6], to(count - 1)),
        remote(at(high, 1), at(high, 1), s.at[7], r.at[7], to(count - 2)),
    ]
    return on


def finish(copies, on):
    copies[0].wait_send()
    copies[1].wait_send()
    wait_all(copies[2:] + on)


def kernel(
    feat_hbm, w_hbm, text_hbm, gfeat_ref, gweight_ref,
    feat, w, text_in, txt, sums, cols, normed, nt_send, nt, part, part_core, part_far, unit, img,
    grad, gs, g_three, g_four, g_one, g_sum, g_two, gproj, wsend, wx, zsend, wz, fin_y, fin_a, fin_b,
    in_s, ax_s, ax_r, az_s, az_r, bx_s, bx_r, bz_s, bz_r, ts_s, ts_r,
    su_s, su_r, co_s, co_r, nt_s, nt_r, pc_s, pc_r, im_s, im_r,
    gy_s, gy_r, gp_s, gp_r, gc_s, gc_r, wx_s, wx_r, wz_s, wz_r, fy_s, fy_r,
    fax_s, fax_r, faz_s, faz_r, fbx_s, fbx_r, fbz_s, fbz_r,
):
    dp = lax.axis_index("dp")
    mp = lax.axis_index("mp")
    yl = dp // (NX * NZ)
    x = (dp // NZ) % NX
    z = dp % NZ
    yh = mp // 2
    c = mp % 2
    y = yh * NYL + yl
    sib = place(x, y, z, 1 - c)
    y_far = (y + NYL) % NY
    far = place(x, y_far, z, c)
    far_sib = place(x, y_far, z, 1 - c)

    def on_y(k):
        return place(x, (y + k) % NY, z, c)

    def on_yl(k):
        return place(x, yh * NYL + (yl + k) % NYL, z, c)

    def on_x(k):
        return place((x + k) % NX, y, z, c)

    def on_z(k):
        return place(x, y, (z + k) % NZ, c)

    barrier = pltpu.get_barrier_semaphore()
    others = [sib, far_sib]
    others += [on_y(k) for k in range(1, NY)]
    others += [on_x(k) for k in range(1, NX)]
    others += [on_z(k) for k in range(1, NZ)]
    for other in others:
        pl.semaphore_signal(barrier, inc=1, device_id=other, device_id_type=MESH)

    text_load = pltpu.make_async_copy(text_hbm, text_in, in_s.at[0])
    feat_load = pltpu.make_async_copy(feat_hbm, feat, in_s.at[1])
    w_load = pltpu.make_async_copy(w_hbm, w, in_s.at[2])
    feat_load.start()
    text_load.start()
    w_load.start()

    feat_load.wait()
    inputs = feat[...].astype(jnp.float32)
    row_sum = jnp.sum(inputs, axis=1, keepdims=True)
    sums[mp] = jnp.broadcast_to(row_sum, (128, 128)).T[:8]
    text_load.wait()
    text = text_in[...].astype(jnp.float32)
    own_text = (text * unit_scale(text)).astype(jnp.bfloat16)
    txt[c, 0, z * NX + x] = own_text[:16]
    txt[c, 1, x * NZ + z] = own_text[16:]
    pl.semaphore_wait(barrier, len(others))

    mates = [sib, far, far_sib]
    sum_copies = [remote(sums.at[mp], sums.at[mp], su_s.at[k], su_r.at[k], to) for k, to in enumerate(mates)]

    own_a = txt.at[c, 0, z * NX + x]
    a_x = [remote(own_a, own_a, ax_s.at[k - 1], ax_r.at[k - 1], on_x(k)) for k in range(1, NX)]

    def b_at(slot, half):
        block = txt.at[c, 1, x * NZ + slot]
        if half is None:
            return block
        return block.at[:, pl.ds(0, 640)] if half == 0 else block.at[:, pl.ds(640, 512)]

    def a_at(slot, half):
        if half is None:
            return txt.at[c, 0, pl.ds(slot * NX, NX)]
        return txt.at[c, 0, pl.ds(slot * NX + half * (NX // 2), NX // 2)]

    b_z = share(b_at, z, NZ, on_z, bz_s, bz_r)

    w_load.wait()
    weights = w[...]
    cols[mp] = jnp.broadcast_to(
        jnp.sum(weights.astype(jnp.float32), axis=0, keepdims=True), (8, weights.shape[1])
    )

    wait_all(sum_copies)
    total = (sums[0] + sums[1]) + (sums[2] + sums[3])
    mean_in = jnp.broadcast_to(total[:1] / 1536.0, (128, 128)).T[:, :1]
    centred = inputs - mean_in
    normed[...] = centred.astype(jnp.bfloat16)
    wait_all(a_x)
    a_z = share(a_at, z, NZ, on_z, az_s, az_r)
    partial = jnp.dot(normed[...], weights, preferred_element_type=jnp.float32)
    for h in range(2):
        for b in range(2):
            part[b, h] = partial[(h * 2 + b) * 32 : (h * 2 + b + 1) * 32]
    core_copy = remote(part.at[1 - c], part_core, pc_s.at[0], pc_r.at[0], sib)
    b_on = pass_on(b_at, z, NZ, on_z, bz_s, bz_r, b_z)
    core_copy.wait()
    part[c, 1 - yh] += part_core[1 - yh]
    far_copy = remote(part.at[c, 1 - yh], part_far, pc_s.at[1], pc_r.at[1], far)
    turned = centred.T.astype(jnp.bfloat16)
    for g in range(NYL):
        nt_send[g] = turned[g * 96 : (g + 1) * 96]
    nt[yl] = nt_send[yl]
    finish(b_z, b_on)
    own_b = txt.at[c, 1, pl.ds(x * NZ, NZ)]
    b_x = [remote(own_b, own_b, bx_s.at[k - 1], bx_r.at[k - 1], on_x(k)) for k in range(1, NX)]
    far_copy.wait()
    project = part[c, yh] + part_core[yh] + part_far[...]
    inv_norm = unit_scale(project)
    unit_img = project * inv_norm
    unit[...] = unit_img
    img[y] = unit_img.astype(jnp.bfloat16)

    def img_at(slot, half):
        return img.at[slot] if half is None else img.at[slot, pl.ds(half * 16, 16)]

    img_one = share(img_at, y, NY, on_y, im_s, im_r)
    col_copies = [remote(cols.at[mp], cols.at[mp], co_s.at[k], co_r.at[k], to) for k, to in enumerate(mates)]
    nt_copies = [
        remote(nt_send.at[(yl + k) % NYL], nt.at[yl], nt_s.at[k - 1], nt_r.at[k - 1], on_yl(k))
        for k in range(1, NYL)
    ]
    a_on = pass_on(a_at, z, NZ, on_z, az_s, az_r, a_z)
    img_on = pass_on(img_at, y, NY, on_y, im_s, im_r, img_one)
    wait_all(b_x)
    text_b = remote(txt.at[c, 1], txt.at[c, 1], ts_s.at[1], ts_r.at[1], sib)
    finish(a_z, a_on)
    text_a = remote(txt.at[c, 0], txt.at[c, 0], ts_s.at[0], ts_r.at[0], sib)
    grad[...] = jnp.zeros_like(grad)
    finish(img_one, img_on)

    def add_texts(core, way):
        texts = txt[core, way].reshape(NX * NZ * 16, -1)
        images = img[...].reshape(NY * 32, -1)
        score = lax.dot_general(images, texts, NT, preferred_element_type=jnp.float32)
        slope = jax.nn.sigmoid(logit_scale * score + logit_bias).astype(jnp.bfloat16)
        grad[...] += jnp.dot(slope, texts, preferred_element_type=jnp.float32).reshape(grad.shape)

    @pl.loop(0, 2)
    def _(way):
        add_texts(c, way)

    text_a.wait()
    text_b.wait()

    @pl.loop(0, 2)
    def _(way):
        add_texts(1 - c, way)

    for k in (3, 4, 5, 1, 7):
        gs[(y + k) % NY] = grad[(y + k) % NY].astype(jnp.bfloat16)

    def give(src, dst, index, k):
        return remote(src, dst, gy_s.at[index], gy_r.at[index], on_y(k))

    three = [
        give(gs.at[(y + 3) % NY], g_three.at[0], 0, 1),
        give(gs.at[(y + NY - 3) % NY], g_three.at[1], 1, NY - 1),
    ]
    four = [
        give(gs.at[(y + 4) % NY, pl.ds(0, 16)], g_four.at[0], 2, 2),
        give(gs.at[(y + 4) % NY, pl.ds(16, 16)], g_four.at[1], 3, NY - 2),
    ]
    one = [
        give(gs.at[(y + 1) % NY], g_one.at[0], 4, 1),
        give(gs.at[(y + NY - 1) % NY], g_one.at[1], 5, NY - 1),
    ]
    own_b16 = img[y].astype(jnp.float32)
    own_t = jnp.concatenate([txt[c, 0, z * NX + x], txt[c, 1, x * NZ + z]], axis=0).astype(jnp.float32)
    own_logit = logit_scale * jnp.sum(own_b16 * own_t, axis=1, keepdims=True) + logit_bias
    wrong = jax.nn.sigmoid(own_logit).astype(jnp.bfloat16).astype(jnp.float32)
    right = (-jax.nn.sigmoid(-own_logit)).astype(jnp.bfloat16).astype(jnp.float32)
    grad_unit = grad[y] + (right - wrong) * own_t
    wsend[...] = jnp.zeros_like(wsend)
    two = []
    for side, k in ((0, 2), (1, NY - 2)):
        three[side].wait()
        four[side].wait()
        far_sum = grad[(y + k) % NY] + g_three[side].astype(jnp.float32)
        lo, hi = far_sum[:16], far_sum[16:]
        if side == 0:
            lo = lo + g_four[0].astype(jnp.float32)
        else:
            hi = hi + g_four[1].astype(jnp.float32)
        g_sum[side, :16] = lo.astype(jnp.bfloat16)
        g_sum[side, 16:] = hi.astype(jnp.bfloat16)
        two.append(give(g_sum.at[side], g_two.at[side], 6 + side, k))
    wait_all(one + two)
    for side in range(2):
        grad_unit = grad_unit + g_one[side].astype(jnp.float32) + g_two[side].astype(jnp.float32)
    grad_unit = logit_scale * grad_unit
    unit_img = unit[...]
    along = jnp.sum(unit_img * grad_unit, axis=1, keepdims=True)
    gproj[c, y] = (inv_norm * (grad_unit - unit_img * along)).astype(jnp.bfloat16)

    def gp_at(slot, half):
        return gproj.at[c, slot] if half is None else gproj.at[c, slot, pl.ds(half * 16, 16)]

    gp_one = share(gp_at, y, NY, on_y, gp_s, gp_r)
    wait_all(col_copies + nt_copies)
    gp_on = pass_on(gp_at, y, NY, on_y, gp_s, gp_r, gp_one)
    finish(gp_one, gp_on)
    remote(gproj.at[c], gproj.at[c], gc_s.at[0], gc_r.at[0], sib).wait()

    def group_rows(g):
        return jnp.concatenate([gproj[0, g], gproj[1, g], gproj[0, g + NYL], gproj[1, g + NYL]], axis=0)

    weight_part = jnp.dot(nt[0], group_rows(0), preferred_element_type=jnp.float32)
    for g in range(1, NYL):
        weight_part += jnp.dot(nt[g], group_rows(g), preferred_element_type=jnp.float32)
    weight_part = weight_part.astype(jnp.bfloat16)
    slots = tile_slots()
    for i, j, tx, tz, k in slots:
        wsend[tx, tz, k] = weight_part[i * 16 : (i + 1) * 16, j * 128 : (j + 1) * 128]
    wx_copies = [
        remote(wsend.at[(x + k) % NX], wx.at[x], wx_s.at[k - 1], wx_r.at[k - 1], on_x(k)) for k in range(1, NX)
    ]
    wx[x] = wsend[x]
    rows = group_rows(yl)
    grad_normed = lax.dot_general(rows, w[...], NT, preferred_element_type=jnp.float32)
    col = (cols[0] + cols[1]) + (cols[2] + cols[3])
    grad_total = jnp.sum(rows.astype(jnp.float32) * col[:1], axis=1, keepdims=True)
    gfeat_ref[...] = (grad_normed - grad_total / 1536.0).astype(jnp.bfloat16)
    wait_all(wx_copies)
    over_x = wx[0].astype(jnp.float32)
    for k in range(1, NX):
        over_x += wx[k].astype(jnp.float32)
    zsend[...] = over_x.astype(jnp.bfloat16)
    wz_copies = [
        remote(zsend.at[(z + k) % NZ], wz.at[z], wz_s.at[k - 1], wz_r.at[k - 1], on_z(k)) for k in range(1, NZ)
    ]
    wz[z] = zsend[z]
    wait_all(wz_copies)
    over_z = wz[0].astype(jnp.float32)
    for k in range(1, NZ):
        over_z += wz[k].astype(jnp.float32)
    fin_y[yl] = over_z.astype(jnp.bfloat16)
    wait_all(
        [remote(fin_y.at[yl], fin_y.at[yl], fy_s.at[k - 1], fy_r.at[k - 1], on_yl(k)) for k in range(1, NYL)]
    )
    fin_a[z, x] = fin_y[:, 0]
    fin_b[x, z] = fin_y[:, 1]
    fa_x = [
        remote(fin_a.at[z, x], fin_a.at[z, x], fax_s.at[k - 1], fax_r.at[k - 1], on_x(k)) for k in range(1, NX)
    ]

    def fa_at(slot, half):
        return fin_a.at[slot] if half is None else fin_a.at[slot, pl.ds(half * (NX // 2), NX // 2)]

    def fb_at(slot, half):
        return fin_b.at[x, slot] if half is None else fin_b.at[x, slot, pl.ds(half * (NYL // 2), NYL // 2)]

    fb_z = share(fb_at, z, NZ, on_z, fbz_s, fbz_r)
    wait_all(fa_x)
    fa_z = share(fa_at, z, NZ, on_z, faz_s, faz_r)
    fb_on = pass_on(fb_at, z, NZ, on_z, fbz_s, fbz_r, fb_z)
    finish(fb_z, fb_on)
    fb_x = [remote(fin_b.at[x], fin_b.at[x], fbx_s.at[k - 1], fbx_r.at[k - 1], on_x(k)) for k in range(1, NX)]
    fa_on = pass_on(fa_at, z, NZ, on_z, faz_s, faz_r, fa_z)
    finish(fa_z, fa_on)
    wait_all(fb_x)
    for g in range(NYL):
        for i, j, tx, tz, k in slots:
            tile = fin_a[tz, tx, g] if k == 0 else fin_b[tx, tz, g]
            gweight_ref[g * 96 + i * 16 : g * 96 + (i + 1) * 16, j * 128 : (j + 1) * 128] = tile


def shards(features, proj_weight, texts):
    rows, width = features.shape
    e = proj_weight.shape[1]
    bf16, f32 = jnp.bfloat16, jnp.float32
    dma = pltpu.SemaphoreType.DMA
    counts = [NX - 1, 8, NX - 1, 8, 2, 3, 3, NYL - 1, 2, 8, 8, 8, 1, NX - 1, NZ - 1, NYL - 1, NX - 1, 8, NX - 1, 8]
    semaphores = [dma((3,))] + [dma((n,)) for n in counts for _ in range(2)]
    hbm = pl.BlockSpec(memory_space=pltpu.HBM)
    grad_features, grad_weight = pl.pallas_call(
        kernel,
        out_shape=(
            jax.ShapeDtypeStruct((rows, width), bf16),
            jax.ShapeDtypeStruct((width, e), bf16),
        ),
        in_specs=[hbm] * 3,
        out_specs=[pl.BlockSpec(memory_space=pltpu.VMEM)] * 2,
        scratch_shapes=[
            pltpu.VMEM((rows, width), bf16),
            pltpu.VMEM((width, e), bf16),
            pltpu.VMEM((32, e), bf16),
            pltpu.VMEM((2, 2, NX * NZ, 16, e), bf16),
            pltpu.VMEM((4, 8, 128), f32),
            pltpu.VMEM((4, 8, e), f32),
            pltpu.VMEM((rows, width), bf16),
            pltpu.VMEM((NYL, width // NYL, rows), bf16),
            pltpu.VMEM((NYL, width // NYL, rows), bf16),
            pltpu.VMEM((2, 2, 32, e), f32),
            pltpu.VMEM((2, 32, e), f32),
            pltpu.VMEM((32, e), f32),
            pltpu.VMEM((32, e), f32),
            pltpu.VMEM((NY, 32, e), bf16),
            pltpu.VMEM((NY, 32, e), f32),
            pltpu.VMEM((NY, 32, e), bf16),
            pltpu.VMEM((2, 32, e), bf16),
            pltpu.VMEM((2, 16, e), bf16),
            pltpu.VMEM((2, 32, e), bf16),
            pltpu.VMEM((2, 32, e), bf16),
            pltpu.VMEM((2, 32, e), bf16),
            pltpu.VMEM((2, NY, 32, e), bf16),
            pltpu.VMEM((NX, NZ, 2, 16, 128), bf16),
            pltpu.VMEM((NX, NZ, 2, 16, 128), bf16),
            pltpu.VMEM((NZ, 2, 16, 128), bf16),
            pltpu.VMEM((NZ, 2, 16, 128), bf16),
            pltpu.VMEM((NYL, 2, 16, 128), bf16),
            pltpu.VMEM((NZ, NX, NYL, 16, 128), bf16),
            pltpu.VMEM((NX, NZ, NYL, 16, 128), bf16),
        ]
        + semaphores,
        compiler_params=pltpu.CompilerParams(
            collective_id=0, has_side_effects=True, vmem_limit_bytes=60 << 20
        ),
        cost_estimate=pl.CostEstimate(flops=2_750_000_000, bytes_accessed=8_000_000, transcendentals=524288),
        name="head_loss",
    )(features, proj_weight, texts)
    return grad_features, grad_weight.astype(f32)


def solution(mesh):
    return jax.shard_map(
        shards,
        mesh=mesh,
        in_specs=(P("dp", "mp"), P("mp", None), P(("dp", "mp"), None)),
        out_specs=(P("dp", "mp"), P("mp", None)),
        check_vma=False,
    )
```

time: 137 us -> 115 us (0.84)
  Pallas kernels: 131 us -> 111 us
  local copies, waits for them, and re-layouts: 3.58 us -> 0.64 us
    pallas_call x1, Pallas kernels: 131 us -> 111 us  [shards(): pl.pallas_call(kernel, out_shape=(jax.ShapeDtypeStruct((rows, width), bf1...]
    unnamed x7 -> x3, local copies, waits for them, and re-layouts: 3.58 us -> 0.64 us
where the time goes in v2:
time: 115 us
  Pallas kernels  111 us (97%)
  other arithmetic  2.52 us (2%)
    pallas_call x1, Pallas kernels, shards(): pl.pallas_call(kernel, out_shape=(jax.ShapeDtypeStruct((rows, width), bf1...  111 us
    convert_element_type x1, other arithmetic, shards(): return (grad_features, grad_weight.astype(f32))  2.52 us

profile of v2, /device:TPU:8, one launch (start us, length us, event | category | flops | bytes accessed | tf_op | source)
XLA Modules:
  0.0 114.6 jit_solution(6803579510697366091)
XLA Ops:
  0.6 110.7 %head_loss.1 = (bf16[128,384]{1,0:T(8,128)(2,1)}, bf16[384,1152]{1,0:T(8,128)(2,1)}) custom-call(bf16[128,384]{1,0:T(8,128)(2,1)} %feat_hbm.1, bf16[384,1152]{1,0:T(8,128)(2,1)} %w_hbm.1, bf16[32,1152]{1,0:T(8,128)(2,1)} %text_hbm.1), custom_call_target="tpu_custom_call" | custom-call | flops 2750000128 | bytes 8000000 | tf_op jit(solution)/shard_map/head_loss/pallas_call | solution.py:353
  111.4 0.0 copy-start
  111.4 2.5 %convert_element_type.3 = f32[384,1152]{1,0:T(8,128)} convert(bf16[384,1152]{1,0:T(8,128)(2,1)} %get-tuple-element.5) | non-fusion elementwise | flops 442368 | bytes 2654208 | tf_op jit(solution)/shard_map/convert_element_type | solution.py:399
  113.9 0.0 copy-done
  113.9 0.6 copy.6
Async XLA Ops:
  111.4 2.5 %copy-start = (bf16[128,384]{1,0:T(8,128)(2,1)S(1)}, bf16[128,384]{1,0:T(8,128)(2,1)}, u32[]{:S(2)}) copy-start(bf16[128,384]{1,0:T(8,128)(2,1)} %get-tuple-element.8) | copy-start | bytes 294916

commit v3 on v2

--- a/solution.py
+++ b/solution.py
@@ -44,38 +44,44 @@
         copy.wait()
 
 
-def share(at, me, count, to, s, r):
+HERE = 2
+
+
+def share(at, ring, to, s, r):
     def go(index, k):
-        return remote(at(me, None), at(me, None), s.at[index], r.at[index], to(k))
-
-    return [go(0, 2), go(1, count - 2), go(2, 1), go(3, count - 1)]
-
-
-def pass_on(at, me, count, to, s, r, copies):
-    low = (me + count - 2) % count
-    high = (me + 2) % count
+        return remote(at(HERE, None), at((HERE - k) % ring, None), s.at[index], r.at[index], to(k % ring))
+
+    return [go(0, 2), go(1, -2), go(2, 1), go(3, -1)]
+
+
+def pass_on(at, ring, to, s, r, copies):
     copies[0].wait_recv()
     on = [
-        remote(at(low, None), at(low, None), s.at[4], r.at[4], to(1)),
-        remote(at(low, 0), at(low, 0), s.at[5], r.at[5], to(2)),
+        remote(at(0, None), at(7, None), s.at[4], r.at[4], to(1)),
+        remote(at(0, 0), at(6, 0), s.at[5], r.at[5], to(2)),
     ]
     copies[1].wait_recv()
     on += [
-        remote(at(high, None), at(high, None), s.at[6], r.at[6], to(count - 1)),
-        remote(at(high, 1), at(high, 1), s.at[7], r.at[7], to(count - 2)),
+        remote(at(4, None), at(5, None), s.at[6], r.at[6], to(ring - 1)),
+        remote(at(4, 1), at(6, 1), s.at[7], r.at[7], to(ring - 2)),
     ]
     return on
+
+
+def near(copies):
+    copies[2].wait()
+    copies[3].wait()
 
 
 def finish(copies, on):
     copies[0].wait_send()
     copies[1].wait_send()
-    wait_all(copies[2:] + on)
+    wait_all(on)
 
 
 def kernel(
     feat_hbm, w_hbm, text_hbm, gfeat_ref, gweight_ref,
-    feat, w, text_in, txt, sums, cols, normed, nt_send, nt, part, part_core, part_far, unit, img,
+    feat, w, text_in, txa, txb, sums, cols, normed, nt_send, nt, part, part_core, part_far, unit, img,
     grad, gs, g_three, g_four, g_one, g_sum, g_two, gproj, wsend, wx, zsend, wz, fin_y, fin_a, fin_b,
     in_s, ax_s, ax_r, az_s, az_r, bx_s, bx_r, bz_s, bz_r, ts_s, ts_r,
     su_s, su_r, co_s, co_r, nt_s, nt_r, pc_s, pc_r, im_s, im_r,
@@ -129,28 +135,34 @@
     text_load.wait()
     text = text_in[...].astype(jnp.float32)
     own_text = (text * unit_scale(text)).astype(jnp.bfloat16)
-    txt[c, 0, z * NX + x] = own_text[:16]
-    txt[c, 1, x * NZ + z] = own_text[16:]
+    txa[c, HERE, x] = own_text[:16]
+    txb[c, x, HERE] = own_text[16:]
     pl.semaphore_wait(barrier, len(others))
 
     mates = [sib, far, far_sib]
     sum_copies = [remote(sums.at[mp], sums.at[mp], su_s.at[k], su_r.at[k], to) for k, to in enumerate(mates)]
 
-    own_a = txt.at[c, 0, z * NX + x]
+    own_a = txa.at[c, HERE, x]
     a_x = [remote(own_a, own_a, ax_s.at[k - 1], ax_r.at[k - 1], on_x(k)) for k in range(1, NX)]
 
-    def b_at(slot, half):
-        block = txt.at[c, 1, x * NZ + slot]
+    def a_at(r, half):
+        return txa.at[c, r] if half is None else txa.at[c, r, pl.ds(half * (NX // 2), NX // 2)]
+
+    def b_at(r, half):
         if half is None:
-            return block
-        return block.at[:, pl.ds(0, 640)] if half == 0 else block.at[:, pl.ds(640, 512)]
-
-    def a_at(slot, half):
-        if half is None:
-            return txt.at[c, 0, pl.ds(slot * NX, NX)]
-        return txt.at[c, 0, pl.ds(slot * NX + half * (NX // 2), NX // 2)]
-
-    b_z = share(b_at, z, NZ, on_z, bz_s, bz_r)
+            return txb.at[c, x, r]
+        return txb.at[c, x, r, :, pl.ds(0, 640)] if half == 0 else txb.at[c, x, r, :, pl.ds(640, 512)]
+
+    def b_to_x(lo, count, index):
+        block = txb.at[c, x, pl.ds(lo, count)]
+        return [
+            remote(block, block, bx_s.at[index + k - 1], bx_r.at[index + k - 1], on_x(k)) for k in range(1, NX)
+        ]
+
+    def to_sib(block, index):
+        return remote(block, block, ts_s.at[index], ts_r.at[index], sib)
+
+    b_z = share(b_at, NZ, on_z, bz_s, bz_r)
 
     w_load.wait()
     weights = w[...]
@@ -158,102 +170,97 @@
         jnp.sum(weights.astype(jnp.float32), axis=0, keepdims=True), (8, weights.shape[1])
     )
 
+    wait_all(a_x)
+    a_z = share(a_at, NZ, on_z, az_s, az_r)
     wait_all(sum_copies)
     total = (sums[0] + sums[1]) + (sums[2] + sums[3])
     mean_in = jnp.broadcast_to(total[:1] / 1536.0, (128, 128)).T[:, :1]
     centred = inputs - mean_in
     normed[...] = centred.astype(jnp.bfloat16)
-    wait_all(a_x)
-    a_z = share(a_at, z, NZ, on_z, az_s, az_r)
     partial = jnp.dot(normed[...], weights, preferred_element_type=jnp.float32)
     for h in range(2):
         for b in range(2):
             part[b, h] = partial[(h * 2 + b) * 32 : (h * 2 + b + 1) * 32]
     core_copy = remote(part.at[1 - c], part_core, pc_s.at[0], pc_r.at[0], sib)
-    b_on = pass_on(b_at, z, NZ, on_z, bz_s, bz_r, b_z)
+    b_on = pass_on(b_at, NZ, on_z, bz_s, bz_r, b_z)
     core_copy.wait()
     part[c, 1 - yh] += part_core[1 - yh]
     far_copy = remote(part.at[c, 1 - yh], part_far, pc_s.at[1], pc_r.at[1], far)
+    near(b_z)
+    b_x = b_to_x(0, 5, 0)
     turned = centred.T.astype(jnp.bfloat16)
     for g in range(NYL):
         nt_send[g] = turned[g * 96 : (g + 1) * 96]
     nt[yl] = nt_send[yl]
+    a_on = pass_on(a_at, NZ, on_z, az_s, az_r, a_z)
     finish(b_z, b_on)
-    own_b = txt.at[c, 1, pl.ds(x * NZ, NZ)]
-    b_x = [remote(own_b, own_b, bx_s.at[k - 1], bx_r.at[k - 1], on_x(k)) for k in range(1, NX)]
+    b_x2 = b_to_x(5, 3, 3)
     far_copy.wait()
     project = part[c, yh] + part_core[yh] + part_far[...]
     inv_norm = unit_scale(project)
     unit_img = project * inv_norm
     unit[...] = unit_img
-    img[y] = unit_img.astype(jnp.bfloat16)
-
-    def img_at(slot, half):
-        return img.at[slot] if half is None else img.at[slot, pl.ds(half * 16, 16)]
-
-    img_one = share(img_at, y, NY, on_y, im_s, im_r)
+    img[HERE] = unit_img.astype(jnp.bfloat16)
+
+    def img_at(r, half):
+        return img.at[r] if half is None else img.at[r, pl.ds(half * 16, 16)]
+
+    img_one = share(img_at, NY, on_y, im_s, im_r)
+    near(a_z)
+    to_core = [to_sib(txa.at[c, pl.ds(0, 5)], 0)]
+    img_on = pass_on(img_at, NY, on_y, im_s, im_r, img_one)
+    wait_all(b_x)
+    to_core += [to_sib(txb.at[c, :, pl.ds(0, 5)], 1)]
+    finish(a_z, a_on)
+    to_core += [to_sib(txa.at[c, pl.ds(5, 3)], 2)]
+    wait_all(b_x2)
+    to_core += [to_sib(txb.at[c, :, pl.ds(5, 3)], 3)]
+    near(img_one)
+    finish(img_one, img_on)
     col_copies = [remote(cols.at[mp], cols.at[mp], co_s.at[k], co_r.at[k], to) for k, to in enumerate(mates)]
     nt_copies = [
         remote(nt_send.at[(yl + k) % NYL], nt.at[yl], nt_s.at[k - 1], nt_r.at[k - 1], on_yl(k))
         for k in range(1, NYL)
     ]
-    a_on = pass_on(a_at, z, NZ, on_z, az_s, az_r, a_z)
-    img_on = pass_on(img_at, y, NY, on_y, im_s, im_r, img_one)
-    wait_all(b_x)
-    text_b = remote(txt.at[c, 1], txt.at[c, 1], ts_s.at[1], ts_r.at[1], sib)
-    finish(a_z, a_on)
-    text_a = remote(txt.at[c, 0], txt.at[c, 0], ts_s.at[0], ts_r.at[0], sib)
-    grad[...] = jnp.zeros_like(grad)
-    finish(img_one, img_on)
-
-    def add_texts(core, way):
-        texts = txt[core, way].reshape(NX * NZ * 16, -1)
+
+    def add_texts(block, first):
+        texts = block[...].reshape(NX * NZ * 16, -1)
         images = img[...].reshape(NY * 32, -1)
         score = lax.dot_general(images, texts, NT, preferred_element_type=jnp.float32)
         slope = jax.nn.sigmoid(logit_scale * score + logit_bias).astype(jnp.bfloat16)
-        grad[...] += jnp.dot(slope, texts, preferred_element_type=jnp.float32).reshape(grad.shape)
-
-    @pl.loop(0, 2)
-    def _(way):
-        add_texts(c, way)
-
-    text_a.wait()
-    text_b.wait()
-
-    @pl.loop(0, 2)
-    def _(way):
-        add_texts(1 - c, way)
-
-    for k in (3, 4, 5, 1, 7):
-        gs[(y + k) % NY] = grad[(y + k) % NY].astype(jnp.bfloat16)
+        terms = jnp.dot(slope, texts, preferred_element_type=jnp.float32).reshape(grad.shape)
+        grad[...] = terms if first else grad[...] + terms
+
+    add_texts(txa.at[c], True)
+    add_texts(txb.at[c], False)
+    wait_all(to_core)
+    add_texts(txa.at[1 - c], False)
+    add_texts(txb.at[1 - c], False)
+
+    for r in (5, 7, 6, 3, 1):
+        gs[r] = grad[r].astype(jnp.bfloat16)
 
     def give(src, dst, index, k):
         return remote(src, dst, gy_s.at[index], gy_r.at[index], on_y(k))
 
-    three = [
-        give(gs.at[(y + 3) % NY], g_three.at[0], 0, 1),
-        give(gs.at[(y + NY - 3) % NY], g_three.at[1], 1, NY - 1),
-    ]
+    three = [give(gs.at[5], g_three.at[0], 0, 1), give(gs.at[7], g_three.at[1], 1, NY - 1)]
     four = [
-        give(gs.at[(y + 4) % NY, pl.ds(0, 16)], g_four.at[0], 2, 2),
-        give(gs.at[(y + 4) % NY, pl.ds(16, 16)], g_four.at[1], 3, NY - 2),
-    ]
-    one = [
-        give(gs.at[(y + 1) % NY], g_one.at[0], 4, 1),
-        give(gs.at[(y + NY - 1) % NY], g_one.at[1], 5, NY - 1),
-    ]
-    own_b16 = img[y].astype(jnp.float32)
-    own_t = jnp.concatenate([txt[c, 0, z * NX + x], txt[c, 1, x * NZ + z]], axis=0).astype(jnp.float32)
+        give(gs.at[6, pl.ds(0, 16)], g_four.at[0], 2, 2),
+        give(gs.at[6, pl.ds(16, 16)], g_four.at[1], 3, NY - 2),
+    ]
+    one = [give(gs.at[3], g_one.at[0], 4, 1), give(gs.at[1], g_one.at[1], 5, NY - 1)]
+    own_b16 = img[HERE].astype(jnp.float32)
+    own_t = jnp.concatenate([txa[c, HERE, x], txb[c, x, HERE]], axis=0).astype(jnp.float32)
     own_logit = logit_scale * jnp.sum(own_b16 * own_t, axis=1, keepdims=True) + logit_bias
     wrong = jax.nn.sigmoid(own_logit).astype(jnp.bfloat16).astype(jnp.float32)
     right = (-jax.nn.sigmoid(-own_logit)).astype(jnp.bfloat16).astype(jnp.float32)
-    grad_unit = grad[y] + (right - wrong) * own_t
+    grad_unit = grad[HERE] + (right - wrong) * own_t
     wsend[...] = jnp.zeros_like(wsend)
     two = []
     for side, k in ((0, 2), (1, NY - 2)):
         three[side].wait()
         four[side].wait()
-        far_sum = grad[(y + k) % NY] + g_three[side].astype(jnp.float32)
+        far_sum = grad[(HERE + k) % NY] + g_three[side].astype(jnp.float32)
         lo, hi = far_sum[:16], far_sum[16:]
         if side == 0:
             lo = lo + g_four[0].astype(jnp.float32)
@@ -268,19 +275,27 @@
     grad_unit = logit_scale * grad_unit
     unit_img = unit[...]
     along = jnp.sum(unit_img * grad_unit, axis=1, keepdims=True)
-    gproj[c, y] = (inv_norm * (grad_unit - unit_img * along)).astype(jnp.bfloat16)
-
-    def gp_at(slot, half):
-        return gproj.at[c, slot] if half is None else gproj.at[c, slot, pl.ds(half * 16, 16)]
-
-    gp_one = share(gp_at, y, NY, on_y, gp_s, gp_r)
+    gproj[c, HERE] = (inv_norm * (grad_unit - unit_img * along)).astype(jnp.bfloat16)
+
+    def gp_at(r, half):
+        return gproj.at[c, r] if half is None else gproj.at[c, r, pl.ds(half * 16, 16)]
+
+    def gp_to_sib(lo, count, index):
+        block = gproj.at[c, pl.ds(lo, count)]
+        return remote(block, block, gc_s.at[index], gc_r.at[index], sib)
+
+    gp_one = share(gp_at, NY, on_y, gp_s, gp_r)
     wait_all(col_copies + nt_copies)
-    gp_on = pass_on(gp_at, y, NY, on_y, gp_s, gp_r, gp_one)
+    gp_on = pass_on(gp_at, NY, on_y, gp_s, gp_r, gp_one)
+    near(gp_one)
+    gp_core = [gp_to_sib(0, 5, 0)]
     finish(gp_one, gp_on)
-    remote(gproj.at[c], gproj.at[c], gc_s.at[0], gc_r.at[0], sib).wait()
+    gp_core += [gp_to_sib(5, 3, 1)]
+    wait_all(gp_core)
 
     def group_rows(g):
-        return jnp.concatenate([gproj[0, g], gproj[1, g], gproj[0, g + NYL], gproj[1, g + NYL]], axis=0)
+        low, high = (g - y + HERE + NY) % NY, (g - y + HERE + NY + NYL) % NY
+        return jnp.concatenate([gproj[0, low], gproj[1, low], gproj[0, high], gproj[1, high]], axis=0)
 
     weight_part = jnp.dot(nt[0], group_rows(0), preferred_element_type=jnp.float32)
     for g in range(1, NYL):
@@ -315,30 +330,39 @@
     wait_all(
         [remote(fin_y.at[yl], fin_y.at[yl], fy_s.at[k - 1], fy_r.at[k - 1], on_yl(k)) for k in range(1, NYL)]
     )
-    fin_a[z, x] = fin_y[:, 0]
-    fin_b[x, z] = fin_y[:, 1]
-    fa_x = [
-        remote(fin_a.at[z, x], fin_a.at[z, x], fax_s.at[k - 1], fax_r.at[k - 1], on_x(k)) for k in range(1, NX)
-    ]
-
-    def fa_at(slot, half):
-        return fin_a.at[slot] if half is None else fin_a.at[slot, pl.ds(half * (NX // 2), NX // 2)]
-
-    def fb_at(slot, half):
-        return fin_b.at[x, slot] if half is None else fin_b.at[x, slot, pl.ds(half * (NYL // 2), NYL // 2)]
-
-    fb_z = share(fb_at, z, NZ, on_z, fbz_s, fbz_r)
+    fin_a[HERE, x] = fin_y[:, 0]
+    fin_b[x, HERE] = fin_y[:, 1]
+    own_fa = fin_a.at[HERE, x]
+    fa_x = [remote(own_fa, own_fa, fax_s.at[k - 1], fax_r.at[k - 1], on_x(k)) for k in range(1, NX)]
+
+    def fa_at(r, half):
+        return fin_a.at[r] if half is None else fin_a.at[r, pl.ds(half * (NX // 2), NX // 2)]
+
+    def fb_at(r, half):
+        return fin_b.at[x, r] if half is None else fin_b.at[x, r, pl.ds(half * (NYL // 2), NYL // 2)]
+
+    def fb_to_x(lo, count, index):
+        block = fin_b.at[x, pl.ds(lo, count)]
+        return [
+            remote(block, block, fbx_s.at[index + k - 1], fbx_r.at[index + k - 1], on_x(k)) for k in range(1, NX)
+        ]
+
+    fb_z = share(fb_at, NZ, on_z, fbz_s, fbz_r)
     wait_all(fa_x)
-    fa_z = share(fa_at, z, NZ, on_z, faz_s, faz_r)
-    fb_on = pass_on(fb_at, z, NZ, on_z, fbz_s, fbz_r, fb_z)
+    fa_z = share(fa_at, NZ, on_z, faz_s, faz_r)
+    fb_on = pass_on(fb_at, NZ, on_z, fbz_s, fbz_r, fb_z)
+    near(fb_z)
+    fb_x = fb_to_x(0, 5, 0)
+    fa_on = pass_on(fa_at, NZ, on_z, faz_s, faz_r, fa_z)
     finish(fb_z, fb_on)
-    fb_x = [remote(fin_b.at[x], fin_b.at[x], fbx_s.at[k - 1], fbx_r.at[k - 1], on_x(k)) for k in range(1, NX)]
-    fa_on = pass_on(fa_at, z, NZ, on_z, faz_s, faz_r, fa_z)
+    fb_x += fb_to_x(5, 3, 3)
+    near(fa_z)
     finish(fa_z, fa_on)
     wait_all(fb_x)
+    at_z = [(tz - z + HERE + NZ) % NZ for tz in range(NZ)]
     for g in range(NYL):
         for i, j, tx, tz, k in slots:
-            tile = fin_a[tz, tx, g] if k == 0 else fin_b[tx, tz, g]
+            tile = fin_a[at_z[tz], tx, g] if k == 0 else fin_b[tx, at_z[tz], g]
             gweight_ref[g * 96 + i * 16 : g * 96 + (i + 1) * 16, j * 128 : (j + 1) * 128] = tile
 
 
@@ -347,7 +371,7 @@
     e = proj_weight.shape[1]
     bf16, f32 = jnp.bfloat16, jnp.float32
     dma = pltpu.SemaphoreType.DMA
-    counts = [NX - 1, 8, NX - 1, 8, 2, 3, 3, NYL - 1, 2, 8, 8, 8, 1, NX - 1, NZ - 1, NYL - 1, NX - 1, 8, NX - 1, 8]
+    counts = [3, 8, 6, 8, 4, 3, 3, NYL - 1, 2, 8, 8, 8, 2, NX - 1, NZ - 1, NYL - 1, 3, 8, 6, 8]
     semaphores = [dma((3,))] + [dma((n,)) for n in counts for _ in range(2)]
     hbm = pl.BlockSpec(memory_space=pltpu.HBM)
     grad_features, grad_weight = pl.pallas_call(
@@ -362,7 +386,8 @@
             pltpu.VMEM((rows, width), bf16),
             pltpu.VMEM((width, e), bf16),
             pltpu.VMEM((32, e), bf16),
-            pltpu.VMEM((2, 2, NX * NZ, 16, e), bf16),
+            pltpu.VMEM((2, NZ, NX, 16, e), bf16),
+            pltpu.VMEM((2, NX, NZ, 16, e), bf16),
             pltpu.VMEM((4, 8, 128), f32),
             pltpu.VMEM((4, 8, e), f32),
             pltpu.VMEM((rows, width), bf16),

time: 115 us -> 107 us (0.930)
  the two profiles are of different devices: /device:TPU:8 before, /device:TPU:4 now
where the time goes in v3:
time: 107 us
  Pallas kernels  103 us (96%)
  other arithmetic  2.52 us (2%)
    pallas_call x1, Pallas kernels, shards(): pl.pallas_call(kernel, out_shape=(jax.ShapeDtypeStruct((rows, width), bf1...  103 us
    convert_element_type x1, other arithmetic, shards(): return (grad_features, grad_weight.astype(f32))  2.52 us

profile of v3, /device:TPU:4, one launch (start us, length us, event | category | flops | bytes accessed | tf_op | source)
XLA Modules:
  0.0 107.0 jit_solution(8234346923114967606)
XLA Ops:
  0.6 103.2 %head_loss.1 = (bf16[128,384]{1,0:T(8,128)(2,1)}, bf16[384,1152]{1,0:T(8,128)(2,1)}) custom-call(bf16[128,384]{1,0:T(8,128)(2,1)} %feat_hbm.1, bf16[384,1152]{1,0:T(8,128)(2,1)} %w_hbm.1, bf16[32,1152]{1,0:T(8,128)(2,1)} %text_hbm.1), custom_call_target="tpu_custom_call" | custom-call | flops 2750000128 | bytes 8000000 | tf_op jit(solution)/shard_map/head_loss/pallas_call | solution.py:377
  103.8 0.0 copy-start
  103.8 2.5 %convert_element_type.3 = f32[384,1152]{1,0:T(8,128)} convert(bf16[384,1152]{1,0:T(8,128)(2,1)} %get-tuple-element.5) | non-fusion elementwise | flops 442368 | bytes 2654208 | tf_op jit(solution)/shard_map/convert_element_type | solution.py:424
  106.3 0.0 copy-done
  106.4 0.6 copy.6
Async XLA Ops:
  103.8 2.5 %copy-start = (bf16[128,384]{1,0:T(8,128)(2,1)S(1)}, bf16[128,384]{1,0:T(8,128)(2,1)}, u32[]{:S(2)}) copy-start(bf16[128,384]{1,0:T(8,128)(2,1)} %get-tuple-element.8) | copy-start | bytes 294916

commit v4 on v3

--- a/solution.py
+++ b/solution.py
@@ -81,7 +81,7 @@
 
 def kernel(
     feat_hbm, w_hbm, text_hbm, gfeat_ref, gweight_ref,
-    feat, w, text_in, txa, txb, sums, cols, normed, nt_send, nt, part, part_core, part_far, unit, img,
+    feat, w, text_in, txa, txb, sums, cols, nt_send, nt, part, part_core, part_far, unit, img,
     grad, gs, g_three, g_four, g_one, g_sum, g_two, gproj, wsend, wx, zsend, wz, fin_y, fin_a, fin_b,
     in_s, ax_s, ax_r, az_s, az_r, bx_s, bx_r, bz_s, bz_r, ts_s, ts_r,
     su_s, su_r, co_s, co_r, nt_s, nt_r, pc_s, pc_r, im_s, im_r,
@@ -125,13 +125,22 @@
     feat_load = pltpu.make_async_copy(feat_hbm, feat, in_s.at[1])
     w_load = pltpu.make_async_copy(w_hbm, w, in_s.at[2])
     feat_load.start()
+    w_load.start()
     text_load.start()
-    w_load.start()
-
+
+    e = w.shape[1]
     feat_load.wait()
     inputs = feat[...].astype(jnp.float32)
-    row_sum = jnp.sum(inputs, axis=1, keepdims=True)
-    sums[mp] = jnp.broadcast_to(row_sum, (128, 128)).T[:8]
+    row_sum = jnp.broadcast_to(jnp.sum(inputs, axis=1, keepdims=True), (128, 128))
+    sums[mp] = row_sum.T[:8]
+    w_load.wait()
+    partial = jnp.dot(feat[...], w[...], preferred_element_type=jnp.float32)
+    for h in range(2):
+        for b in range(2):
+            lo = (h * 2 + b) * 32
+            part[b, h, :, :e] = partial[lo : lo + 32]
+            part[b, h, :, e:] = row_sum[lo : lo + 32]
+    cols[mp] = jnp.sum(w[...].astype(jnp.float32), axis=0, keepdims=True)
     text_load.wait()
     text = text_in[...].astype(jnp.float32)
     own_text = (text * unit_scale(text)).astype(jnp.bfloat16)
@@ -139,8 +148,9 @@
     txb[c, x, HERE] = own_text[16:]
     pl.semaphore_wait(barrier, len(others))
 
+    core_copy = remote(part.at[1 - c], part_core, pc_s.at[0], pc_r.at[0], sib)
     mates = [sib, far, far_sib]
-    sum_copies = [remote(sums.at[mp], sums.at[mp], su_s.at[k], su_r.at[k], to) for k, to in enumerate(mates)]
+    col_copies = [remote(cols.at[mp], cols.at[mp], co_s.at[k], co_r.at[k], to) for k, to in enumerate(mates)]
 
     own_a = txa.at[c, HERE, x]
     a_x = [remote(own_a, own_a, ax_s.at[k - 1], ax_r.at[k - 1], on_x(k)) for k in range(1, NX)]
@@ -164,39 +174,21 @@
 
     b_z = share(b_at, NZ, on_z, bz_s, bz_r)
 
-    w_load.wait()
-    weights = w[...]
-    cols[mp] = jnp.broadcast_to(
-        jnp.sum(weights.astype(jnp.float32), axis=0, keepdims=True), (8, weights.shape[1])
-    )
-
-    wait_all(a_x)
-    a_z = share(a_at, NZ, on_z, az_s, az_r)
-    wait_all(sum_copies)
-    total = (sums[0] + sums[1]) + (sums[2] + sums[3])
-    mean_in = jnp.broadcast_to(total[:1] / 1536.0, (128, 128)).T[:, :1]
-    centred = inputs - mean_in
-    normed[...] = centred.astype(jnp.bfloat16)
-    partial = jnp.dot(normed[...], weights, preferred_element_type=jnp.float32)
-    for h in range(2):
-        for b in range(2):
-            part[b, h] = partial[(h * 2 + b) * 32 : (h * 2 + b + 1) * 32]
-    core_copy = remote(part.at[1 - c], part_core, pc_s.at[0], pc_r.at[0], sib)
-    b_on = pass_on(b_at, NZ, on_z, bz_s, bz_r, b_z)
+    sum_copies = [remote(sums.at[mp], sums.at[mp], su_s.at[k], su_r.at[k], to) for k, to in enumerate(mates)]
+
     core_copy.wait()
     part[c, 1 - yh] += part_core[1 - yh]
     far_copy = remote(part.at[c, 1 - yh], part_far, pc_s.at[1], pc_r.at[1], far)
+    wait_all(a_x)
+    a_z = share(a_at, NZ, on_z, az_s, az_r)
+    b_on = pass_on(b_at, NZ, on_z, bz_s, bz_r, b_z)
     near(b_z)
     b_x = b_to_x(0, 5, 0)
-    turned = centred.T.astype(jnp.bfloat16)
-    for g in range(NYL):
-        nt_send[g] = turned[g * 96 : (g + 1) * 96]
-    nt[yl] = nt_send[yl]
-    a_on = pass_on(a_at, NZ, on_z, az_s, az_r, a_z)
-    finish(b_z, b_on)
-    b_x2 = b_to_x(5, 3, 3)
+    wait_all(col_copies)
+    col = (cols[0] + cols[1]) + (cols[2] + cols[3])
     far_copy.wait()
-    project = part[c, yh] + part_core[yh] + part_far[...]
+    joined = part[c, yh] + part_core[yh] + part_far[...]
+    project = joined[:, :e] - (joined[:, e : e + 1] / 1536.0) * col
     inv_norm = unit_scale(project)
     unit_img = project * inv_norm
     unit[...] = unit_img
@@ -206,18 +198,27 @@
         return img.at[r] if half is None else img.at[r, pl.ds(half * 16, 16)]
 
     img_one = share(img_at, NY, on_y, im_s, im_r)
+    finish(b_z, b_on)
+    b_x2 = b_to_x(5, 3, 3)
+    a_on = pass_on(a_at, NZ, on_z, az_s, az_r, a_z)
+    img_on = pass_on(img_at, NY, on_y, im_s, im_r, img_one)
+    wait_all(sum_copies)
+    total = (sums[0] + sums[1]) + (sums[2] + sums[3])
+    mean_in = jnp.broadcast_to(total[:1] / 1536.0, (128, 128)).T[:, :1]
+    turned = (feat[...].astype(jnp.float32) - mean_in).T.astype(jnp.bfloat16)
+    for g in range(NYL):
+        nt_send[g] = turned[g * 96 : (g + 1) * 96]
+    nt[yl] = nt_send[yl]
     near(a_z)
     to_core = [to_sib(txa.at[c, pl.ds(0, 5)], 0)]
-    img_on = pass_on(img_at, NY, on_y, im_s, im_r, img_one)
     wait_all(b_x)
     to_core += [to_sib(txb.at[c, :, pl.ds(0, 5)], 1)]
+    near(img_one)
+    finish(img_one, img_on)
     finish(a_z, a_on)
     to_core += [to_sib(txa.at[c, pl.ds(5, 3)], 2)]
     wait_all(b_x2)
     to_core += [to_sib(txb.at[c, :, pl.ds(5, 3)], 3)]
-    near(img_one)
-    finish(img_one, img_on)
-    col_copies = [remote(cols.at[mp], cols.at[mp], co_s.at[k], co_r.at[k], to) for k, to in enumerate(mates)]
     nt_copies = [
         remote(nt_send.at[(yl + k) % NYL], nt.at[yl], nt_s.at[k - 1], nt_r.at[k - 1], on_yl(k))
         for k in range(1, NYL)
@@ -285,7 +286,7 @@
         return remote(block, block, gc_s.at[index], gc_r.at[index], sib)
 
     gp_one = share(gp_at, NY, on_y, gp_s, gp_r)
-    wait_all(col_copies + nt_copies)
+    wait_all(nt_copies)
     gp_on = pass_on(gp_at, NY, on_y, gp_s, gp_r, gp_one)
     near(gp_one)
     gp_core = [gp_to_sib(0, 5, 0)]
@@ -310,8 +311,7 @@
     wx[x] = wsend[x]
     rows = group_rows(yl)
     grad_normed = lax.dot_general(rows, w[...], NT, preferred_element_type=jnp.float32)
-    col = (cols[0] + cols[1]) + (cols[2] + cols[3])
-    grad_total = jnp.sum(rows.astype(jnp.float32) * col[:1], axis=1, keepdims=True)
+    grad_total = jnp.sum(rows.astype(jnp.float32) * col, axis=1, keepdims=True)
     gfeat_ref[...] = (grad_normed - grad_total / 1536.0).astype(jnp.bfloat16)
     wait_all(wx_copies)
     over_x = wx[0].astype(jnp.float32)
@@ -389,13 +389,12 @@
             pltpu.VMEM((2, NZ, NX, 16, e), bf16),
             pltpu.VMEM((2, NX, NZ, 16, e), bf16),
             pltpu.VMEM((4, 8, 128), f32),
-            pltpu.VMEM((4, 8, e), f32),
-            pltpu.VMEM((rows, width), bf16),
+            pltpu.VMEM((4, 1, e), f32),
             pltpu.VMEM((NYL, width // NYL, rows), bf16),
             pltpu.VMEM((NYL, width // NYL, rows), bf16),
-            pltpu.VMEM((2, 2, 32, e), f32),
-            pltpu.VMEM((2, 32, e), f32),
-            pltpu.VMEM((32, e), f32),
+            pltpu.VMEM((2, 2, 32, e + 128), f32),
+            pltpu.VMEM((2, 32, e + 128), f32),
+            pltpu.VMEM((32, e + 128), f32),
             pltpu.VMEM((32, e), f32),
             pltpu.VMEM((NY, 32, e), bf16),
             pltpu.VMEM((NY, 32, e), f32),

time: 107 us -> 103 us (0.963)
  Pallas kernels: 103 us -> 99.4 us
    pallas_call x1, Pallas kernels: 103 us -> 99.4 us  [shards(): pl.pallas_call(kernel, out_shape=(jax.ShapeDtypeStruct((rows, width), bf1...]
where the time goes in v4:
time: 103 us
  Pallas kernels  99.4 us (97%)
  other arithmetic  2.52 us (2%)
    pallas_call x1, Pallas kernels, shards(): pl.pallas_call(kernel, out_shape=(jax.ShapeDtypeStruct((rows, width), bf1...  99.4 us
    convert_element_type x1, other arithmetic, shards(): return (grad_features, grad_weight.astype(f32))  2.52 us

profile of v4, /device:TPU:4, one launch (start us, length us, event | category | flops | bytes accessed | tf_op | source)
XLA Modules:
  0.0 103.2 jit_solution(11394063877703189729)
XLA Ops:
  0.6 99.4 %head_loss.1 = (bf16[128,384]{1,0:T(8,128)(2,1)}, bf16[384,1152]{1,0:T(8,128)(2,1)}) custom-call(bf16[128,384]{1,0:T(8,128)(2,1)} %feat_hbm.1, bf16[384,1152]{1,0:T(8,128)(2,1)} %w_hbm.1, bf16[32,1152]{1,0:T(8,128)(2,1)} %text_hbm.1), custom_call_target="tpu_custom_call" | custom-call | flops 2750000128 | bytes 8000000 | tf_op jit(solution)/shard_map/head_loss/pallas_call | solution.py:377
  100.0 0.0 copy-start
  100.0 2.5 %convert_element_type.3 = f32[384,1152]{1,0:T(8,128)} convert(bf16[384,1152]{1,0:T(8,128)(2,1)} %get-tuple-element.5) | non-fusion elementwise | flops 442368 | bytes 2654208 | tf_op jit(solution)/shard_map/convert_element_type | solution.py:423
  102.6 0.0 copy-done
  102.6 0.6 copy.6
Async XLA Ops:
  100.0 2.5 %copy-start = (bf16[128,384]{1,0:T(8,128)(2,1)S(1)}, bf16[128,384]{1,0:T(8,128)(2,1)}, u32[]{:S(2)}) copy-start(bf16[128,384]{1,0:T(8,128)(2,1)} %get-tuple-element.8) | copy-start | bytes 294916

commit v5 on v4

--- a/solution.py
+++ b/solution.py
@@ -71,6 +71,22 @@
 def near(copies):
     copies[2].wait()
     copies[3].wait()
+
+
+def relay(step, at, ring, to, s, r, before):
+    copies = {}
+    for piece in range(2):
+        for way, d in enumerate((1, -1)):
+            if step == 4 and piece != way:
+                continue
+            if step > 1:
+                before[piece, way].wait_recv()
+            block = (HERE - d * (step - 1)) % ring
+            index = ((step - 1) * 2 + piece) * 2 + way
+            copies[piece, way] = remote(
+                at(block, piece), at((block - d) % ring, piece), s.at[index], r.at[index], to(d % ring)
+            )
+    return copies
 
 
 def finish(copies, on):
@@ -180,10 +196,11 @@
     part[c, 1 - yh] += part_core[1 - yh]
     far_copy = remote(part.at[c, 1 - yh], part_far, pc_s.at[1], pc_r.at[1], far)
     wait_all(a_x)
-    a_z = share(a_at, NZ, on_z, az_s, az_r)
+    a_1 = relay(1, a_at, NZ, on_z, az_s, az_r, None)
     b_on = pass_on(b_at, NZ, on_z, bz_s, bz_r, b_z)
     near(b_z)
     b_x = b_to_x(0, 5, 0)
+    a_2 = relay(2, a_at, NZ, on_z, az_s, az_r, a_1)
     wait_all(col_copies)
     col = (cols[0] + cols[1]) + (cols[2] + cols[3])
     far_copy.wait()
@@ -200,7 +217,7 @@
     img_one = share(img_at, NY, on_y, im_s, im_r)
     finish(b_z, b_on)
     b_x2 = b_to_x(5, 3, 3)
-    a_on = pass_on(a_at, NZ, on_z, az_s, az_r, a_z)
+    a_3 = relay(3, a_at, NZ, on_z, az_s, az_r, a_2)
     img_on = pass_on(img_at, NY, on_y, im_s, im_r, img_one)
     wait_all(sum_copies)
     total = (sums[0] + sums[1]) + (sums[2] + sums[3])
@@ -209,16 +226,23 @@
     for g in range(NYL):
         nt_send[g] = turned[g * 96 : (g + 1) * 96]
     nt[yl] = nt_send[yl]
-    near(a_z)
     to_core = [to_sib(txa.at[c, pl.ds(0, 5)], 0)]
+    a_4 = relay(4, a_at, NZ, on_z, az_s, az_r, a_3)
     wait_all(b_x)
     to_core += [to_sib(txb.at[c, :, pl.ds(0, 5)], 1)]
+    a_3[1, 0].wait_recv()
+    a_3[0, 1].wait_recv()
+    to_core += [to_sib(txa.at[c, 5], 2), to_sib(txa.at[c, 7], 4)]
     near(img_one)
     finish(img_one, img_on)
-    finish(a_z, a_on)
-    to_core += [to_sib(txa.at[c, pl.ds(5, 3)], 2)]
     wait_all(b_x2)
     to_core += [to_sib(txb.at[c, :, pl.ds(5, 3)], 3)]
+    for copies in (a_1, a_2, a_3, a_4):
+        for copy in copies.values():
+            copy.wait_send()
+    for copy in a_4.values():
+        copy.wait_recv()
+    to_core += [to_sib(txa.at[c, 6], 5)]
     nt_copies = [
         remote(nt_send.at[(yl + k) % NYL], nt.at[yl], nt_s.at[k - 1], nt_r.at[k - 1], on_yl(k))
         for k in range(1, NYL)
@@ -371,7 +395,7 @@
     e = proj_weight.shape[1]
     bf16, f32 = jnp.bfloat16, jnp.float32
     dma = pltpu.SemaphoreType.DMA
-    counts = [3, 8, 6, 8, 4, 3, 3, NYL - 1, 2, 8, 8, 8, 2, NX - 1, NZ - 1, NYL - 1, 3, 8, 6, 8]
+    counts = [3, 16, 6, 8, 6, 3, 3, NYL - 1, 2, 8, 8, 8, 2, NX - 1, NZ - 1, NYL - 1, 3, 8, 6, 8]
     semaphores = [dma((3,))] + [dma((n,)) for n in counts for _ in range(2)]
     hbm = pl.BlockSpec(memory_space=pltpu.HBM)
     grad_features, grad_weight = pl.pallas_call(

time: 103 us -> 102 us (level)
  the two profiles are of different devices: /device:TPU:4 before, /device:TPU:8 now
where the time goes in v5:
time: 102 us
  Pallas kernels  98.3 us (96%)
  other arithmetic  2.52 us (2%)
    pallas_call x1, Pallas kernels, shards(): pl.pallas_call(kernel, out_shape=(jax.ShapeDtypeStruct((rows, width), bf1...  98.3 us
    convert_element_type x1, other arithmetic, shards(): return (grad_features, grad_weight.astype(f32))  2.52 us

profile of v5, /device:TPU:8, one launch (start us, length us, event | category | flops | bytes accessed | tf_op | source)
XLA Modules:
  0.0 102.1 jit_solution(8045621895812237374)
XLA Ops:
  0.6 98.3 %head_loss.1 = (bf16[128,384]{1,0:T(8,128)(2,1)}, bf16[384,1152]{1,0:T(8,128)(2,1)}) custom-call(bf16[128,384]{1,0:T(8,128)(2,1)} %feat_hbm.1, bf16[384,1152]{1,0:T(8,128)(2,1)} %w_hbm.1, bf16[32,1152]{1,0:T(8,128)(2,1)} %text_hbm.1), custom_call_target="tpu_custom_call" | custom-call | flops 2750000128 | bytes 8000000 | tf_op jit(solution)/shard_map/head_loss/pallas_call | solution.py:401
  98.9 0.0 copy-start
  98.9 2.5 %convert_element_type.3 = f32[384,1152]{1,0:T(8,128)} convert(bf16[384,1152]{1,0:T(8,128)(2,1)} %get-tuple-element.5) | non-fusion elementwise | flops 442368 | bytes 2654208 | tf_op jit(solution)/shard_map/convert_element_type | solution.py:447
  101.5 0.0 copy-done
  101.5 0.6 copy.6
Async XLA Ops:
  98.9 2.5 %copy-start = (bf16[128,384]{1,0:T(8,128)(2,1)S(1)}, bf16[128,384]{1,0:T(8,128)(2,1)}, u32[]{:S(2)}) copy-start(bf16[128,384]{1,0:T(8,128)(2,1)} %get-tuple-element.8) | copy-start | bytes 294916

commit v6 on v5

--- a/solution.py
+++ b/solution.py
@@ -98,7 +98,7 @@
 def kernel(
     feat_hbm, w_hbm, text_hbm, gfeat_ref, gweight_ref,
     feat, w, text_in, txa, txb, sums, cols, nt_send, nt, part, part_core, part_far, unit, img,
-    grad, gs, g_three, g_four, g_one, g_sum, g_two, gproj, wsend, wx, zsend, wz, fin_y, fin_a, fin_b,
+    grad, gs, g_three, g_four, g_one, g_sum, g_two, gproj, wsend, wx, zsend, wz, fin_a, fin_b,
     in_s, ax_s, ax_r, az_s, az_r, bx_s, bx_r, bz_s, bz_r, ts_s, ts_r,
     su_s, su_r, co_s, co_r, nt_s, nt_r, pc_s, pc_r, im_s, im_r,
     gy_s, gy_r, gp_s, gp_r, gc_s, gc_r, wx_s, wx_r, wz_s, wz_r, fy_s, fy_r,
@@ -126,6 +126,9 @@
     def on_x(k):
         return place((x + k) % NX, y, z, c)
 
+    def on_yl_x(j, k):
+        return place((x + k) % NX, yh * NYL + (yl + j) % NYL, z, c)
+
     def on_z(k):
         return place(x, y, (z + k) % NZ, c)
 
@@ -134,6 +137,7 @@
     others += [on_y(k) for k in range(1, NY)]
     others += [on_x(k) for k in range(1, NX)]
     others += [on_z(k) for k in range(1, NZ)]
+    others += [on_yl_x(j, k) for j in range(1, NYL) for k in range(1, NX)]
     for other in others:
         pl.semaphore_signal(barrier, inc=1, device_id=other, device_id_type=MESH)
 
@@ -350,14 +354,18 @@
     over_z = wz[0].astype(jnp.float32)
     for k in range(1, NZ):
         over_z += wz[k].astype(jnp.float32)
-    fin_y[yl] = over_z.astype(jnp.bfloat16)
-    wait_all(
-        [remote(fin_y.at[yl], fin_y.at[yl], fy_s.at[k - 1], fy_r.at[k - 1], on_yl(k)) for k in range(1, NYL)]
-    )
-    fin_a[HERE, x] = fin_y[:, 0]
-    fin_b[x, HERE] = fin_y[:, 1]
-    own_fa = fin_a.at[HERE, x]
-    fa_x = [remote(own_fa, own_fa, fax_s.at[k - 1], fax_r.at[k - 1], on_x(k)) for k in range(1, NX)]
+    done = over_z.astype(jnp.bfloat16)
+    fin_a[HERE, x, yl] = done[0]
+    fin_b[x, HERE, yl] = done[1]
+    own_fb = fin_b.at[x, HERE, yl]
+    fb_y = [remote(own_fb, own_fb, fy_s.at[k - 1], fy_r.at[k - 1], on_yl(k)) for k in range(1, NYL)]
+    own_fa = fin_a.at[HERE, x, yl]
+    fa_x = [
+        remote(own_fa, own_fa, fax_s.at[j * NX + k], fax_r.at[j * NX + k], on_yl_x(j, k))
+        for j in range(NYL)
+        for k in range(NX)
+        if j + k > 0
+    ]
 
     def fa_at(r, half):
         return fin_a.at[r] if half is None else fin_a.at[r, pl.ds(half * (NX // 2), NX // 2)]
@@ -371,6 +379,7 @@
             remote(block, block, fbx_s.at[index + k - 1], fbx_r.at[index + k - 1], on_x(k)) for k in range(1, NX)
         ]
 
+    wait_all(fb_y)
     fb_z = share(fb_at, NZ, on_z, fbz_s, fbz_r)
     wait_all(fa_x)
     fa_z = share(fa_at, NZ, on_z, faz_s, faz_r)
@@ -395,7 +404,7 @@
     e = proj_weight.shape[1]
     bf16, f32 = jnp.bfloat16, jnp.float32
     dma = pltpu.SemaphoreType.DMA
-    counts = [3, 16, 6, 8, 6, 3, 3, NYL - 1, 2, 8, 8, 8, 2, NX - 1, NZ - 1, NYL - 1, 3, 8, 6, 8]
+    counts = [3, 16, 6, 8, 6, 3, 3, NYL - 1, 2, 8, 8, 8, 2, NX - 1, NZ - 1, NYL - 1, NYL * NX, 8, 6, 8]
     semaphores = [dma((3,))] + [dma((n,)) for n in counts for _ in range(2)]
     hbm = pl.BlockSpec(memory_space=pltpu.HBM)
     grad_features, grad_weight = pl.pallas_call(
@@ -433,7 +442,6 @@
             pltpu.VMEM((NX, NZ, 2, 16, 128), bf16),
             pltpu.VMEM((NZ, 2, 16, 128), bf16),
             pltpu.VMEM((NZ, 2, 16, 128), bf16),
-            pltpu.VMEM((NYL, 2, 16, 128), bf16),
             pltpu.VMEM((NZ, NX, NYL, 16, 128), bf16),
             pltpu.VMEM((NX, NZ, NYL, 16, 128), bf16),
         ]

time: 102 us -> 101 us (level)
  Pallas kernels: 98.3 us -> 96.6 us
    pallas_call x1, Pallas kernels: 98.3 us -> 96.6 us  [shards(): pl.pallas_call(kernel, out_shape=(jax.ShapeDtypeStruct((rows, width), bf1...]
where the time goes in v6:
time: 101 us; the launch traced here: 100 us
  Pallas kernels  96.6 us (96%)
  other arithmetic  2.52 us (2%)
    pallas_call x1, Pallas kernels, shards(): pl.pallas_call(kernel, out_shape=(jax.ShapeDtypeStruct((rows, width), bf1...  96.6 us
    convert_element_type x1, other arithmetic, shards(): return (grad_features, grad_weight.astype(f32))  2.52 us

profile of v6, /device:TPU:8, one launch (start us, length us, event | category | flops | bytes accessed | tf_op | source)
XLA Modules:
  0.0 100.4 jit_solution(390764415509443674)
XLA Ops:
  0.6 96.6 %head_loss.1 = (bf16[128,384]{1,0:T(8,128)(2,1)}, bf16[384,1152]{1,0:T(8,128)(2,1)}) custom-call(bf16[128,384]{1,0:T(8,128)(2,1)} %feat_hbm.1, bf16[384,1152]{1,0:T(8,128)(2,1)} %w_hbm.1, bf16[32,1152]{1,0:T(8,128)(2,1)} %text_hbm.1), custom_call_target="tpu_custom_call" | custom-call | flops 2750000128 | bytes 8000000 | tf_op jit(solution)/shard_map/head_loss/pallas_call | solution.py:410
  97.3 0.0 copy-start
  97.3 2.5 %convert_element_type.3 = f32[384,1152]{1,0:T(8,128)} convert(bf16[384,1152]{1,0:T(8,128)(2,1)} %get-tuple-element.5) | non-fusion elementwise | flops 442368 | bytes 2654208 | tf_op jit(solution)/shard_map/convert_element_type | solution.py:455
  99.8 0.0 copy-done
  99.8 0.6 copy.6
Async XLA Ops:
  97.3 2.5 %copy-start = (bf16[128,384]{1,0:T(8,128)(2,1)S(1)}, bf16[128,384]{1,0:T(8,128)(2,1)}, u32[]{:S(2)}) copy-start(bf16[128,384]{1,0:T(8,128)(2,1)} %get-tuple-element.8) | copy-start | bytes 294916

commit v7 on v6

--- a/solution.py
+++ b/solution.py
@@ -396,7 +396,7 @@
     for g in range(NYL):
         for i, j, tx, tz, k in slots:
             tile = fin_a[at_z[tz], tx, g] if k == 0 else fin_b[tx, at_z[tz], g]
-            gweight_ref[g * 96 + i * 16 : g * 96 + (i + 1) * 16, j * 128 : (j + 1) * 128] = tile
+            gweight_ref[g * 96 + i * 16 : g * 96 + (i + 1) * 16, j * 128 : (j + 1) * 128] = tile.astype(jnp.float32)
 
 
 def shards(features, proj_weight, texts):
@@ -411,7 +411,7 @@
         kernel,
         out_shape=(
             jax.ShapeDtypeStruct((rows, width), bf16),
-            jax.ShapeDtypeStruct((width, e), bf16),
+            jax.ShapeDtypeStruct((width, e), f32),
         ),
         in_specs=[hbm] * 3,
         out_specs=[pl.BlockSpec(memory_space=pltpu.VMEM)] * 2,
@@ -452,7 +452,7 @@
         cost_estimate=pl.CostEstimate(flops=2_750_000_000, bytes_accessed=8_000_000, transcendentals=524288),
         name="head_loss",
     )(features, proj_weight, texts)
-    return grad_features, grad_weight.astype(f32)
+    return grad_features, grad_weight
 
 
 def solution(mesh):

time: 101 us -> 102 us (level)
  local copies, waits for them, and re-layouts: 0.64 us -> 4.34 us
  other arithmetic: 2.52 us -> 0 us
    unnamed x3 -> x2, local copies, waits for them, and re-layouts: 0.64 us -> 4.34 us
    convert_element_type x1 -> x0, other arithmetic: 2.52 us -> none  [shards(): return (grad_features, grad_weight.astype(f32))]
where the time goes in v7:
time: 102 us
  Pallas kernels  96.9 us (95%)
  local copies, waits for them, and re-layouts  4.34 us (4%)
    pallas_call x1, Pallas kernels, shards(): pl.pallas_call(kernel, out_shape=(jax.ShapeDtypeStruct((rows, width), bf1...  96.9 us
    unnamed x2, local copies, waits for them, and re-layouts  4.34 us

profile of v7, /device:TPU:8, one launch (start us, length us, event | category | flops | bytes accessed | tf_op | source)
XLA Modules:
  0.0 101.8 jit_solution(16469079642354219117)
XLA Ops:
  0.6 96.9 %head_loss.1 = (bf16[128,384]{1,0:T(8,128)(2,1)}, f32[384,1152]{1,0:T(8,128)}) custom-call(bf16[128,384]{1,0:T(8,128)(2,1)} %feat_hbm.1, bf16[384,1152]{1,0:T(8,128)(2,1)} %w_hbm.1, bf16[32,1152]{1,0:T(8,128)(2,1)} %text_hbm.1), custom_call_target="tpu_custom_call" | custom-call | flops 2750000128 | bytes 8000000 | tf_op jit(solution)/shard_map/head_loss/pallas_call | solution.py:410
  97.5 1.5 %copy.7 = bf16[128,384]{1,0:T(8,128)(2,1)} copy(bf16[128,384]{1,0:T(8,128)(2,1)} %get-tuple-element.4) | data formatting | bytes 196608
  99.0 2.8 %copy.8 = f32[384,1152]{1,0:T(8,128)} copy(f32[384,1152]{1,0:T(8,128)} %get-tuple-element.5) | data formatting | bytes 3538944
